TPU v7x, 32 devices: a whole 2x2x4 slice. The times are simulated.
32 devices in a mesh: group: 2 (over x), wide: 16 (over z, y, core).
Axes of the slice: x: 2, y: 2, z: 4, core: 2. Of those that a mesh axis runs over, the one named last changes fastest.
Arguments:
- residual: bfloat16 [64, 16384], P('group', 'wide'), parts along dimension 0, may hold values from -4 to 4
- norm_gain: bfloat16 [16384], P('wide'), may hold values from 0.25 to 1.75
- w_qkv: bfloat16 [16384, 9216], P('wide'), may hold values from -1 to 1
- w_out: bfloat16 [8192, 16384], P(None, 'wide'), may hold values from -16 to 16
- cached_key_rows: bfloat16 [64, 512, 512], P(('group', 'wide')), parts along dimension 0, may hold values from -256 to 256
- cached_value_rows: bfloat16 [64, 512, 512], P(('group', 'wide')), parts along dimension 0, may hold values from -6 to 6
- lengths: int32 [64], P(('group', 'wide')), parts along dimension 0, may hold values from 32 to 512, as said below
Outputs:
- branch: bfloat16 [2, 64, 16384], P(None, 'group', 'wide'), parts along dimension 1
- fresh_kv: bfloat16 [64, 2, 1024], P(('group', 'wide')), parts along dimension 0
There are 2 independent parts, one for each index of `group`. A program takes and returns all parts, laid end to end along the dimension named above; an argument that names none is the same for every part. Nothing has to cross between parts.
Inputs may be any that keep to these rules, and one draw needn't show every extreme that they name: `lengths`: one sequence in every draw fills all 512 slots.
All inputs are finite; a program needn't handle non-finite values.
Results may differ from a plain program's by a relative error of at most 0.019.
Values may be sent and summed in bfloat16 or wider, within the bound.
A program may use at most 128 MiB of HBM per device.

v0:
```python
import jax
import jax.numpy as jnp
from jax import lax
from jax.sharding import PartitionSpec as P

D = 16384
QUERY_HEADS = 64
KEY_VALUE_HEADS = 4
HEAD_SIZE = 128
DECODE_STEPS = 2


EPSILON = 1e-05


def apply_rotation(vectors, token_position):
    half_width = vectors.shape[-1] // 2
    frequency = 500000.0 ** (
        -(jnp.arange(half_width, dtype=jnp.float32) * (2.0 / vectors.shape[-1]))
    )
    angles = token_position.astype(jnp.float32)[:, None, None] * frequency
    cosine = jnp.cos(angles)
    sine_part = jnp.sin(angles)
    first_half = vectors[..., :half_width]
    second_half = vectors[..., half_width:]
    return jnp.concatenate(
        [
            first_half * cosine - second_half * sine_part,
            first_half * sine_part + second_half * cosine,
        ],
        axis=-1,
    )


def attend(query_rows, keys_grouped, values_grouped, lengths, new_keys, new_values):
    scaling = 1.0 / HEAD_SIZE**0.5
    cache_positions = keys_grouped.shape[1]
    cache_scores = (
        jnp.einsum("bkgd,bpkd->bkgp", query_rows, keys_grouped, preferred_element_type=jnp.float32)
        * scaling
    )
    visible = jnp.arange(cache_positions, dtype=jnp.int32)[None, :] < lengths[:, None]
    cache_scores = jnp.where(visible[:, None, None, :], cache_scores, -jnp.inf)
    new_scores = (
        jnp.einsum("bkgd,bktd->bkgt", query_rows, new_keys, preferred_element_type=jnp.float32)
        * scaling
    )
    peak = jnp.maximum(jnp.max(cache_scores, axis=-1), jnp.max(new_scores, axis=-1))
    cache_exp = jnp.exp(cache_scores - peak[..., None])
    new_exp = jnp.exp(new_scores - peak[..., None])
    denominator = jnp.sum(cache_exp, axis=-1) + jnp.sum(new_exp, axis=-1)
    weighted = jnp.einsum(
        "bkgp,bpkd->bkgd",
        cache_exp.astype(jnp.bfloat16),
        values_grouped,
        preferred_element_type=jnp.float32,
    )
    weighted = weighted + jnp.einsum(
        "bkgt,bktd->bkgd",
        new_exp.astype(jnp.bfloat16),
        new_values,
        preferred_element_type=jnp.float32,
    )
    result = (weighted / denominator[..., None]).astype(jnp.bfloat16)
    return result.reshape(result.shape[0], QUERY_HEADS * HEAD_SIZE)


def shards(residual, norm_gain, w_qkv, w_out, cached_key_rows, cached_value_rows, lengths):
    sequence_rows = lengths.shape[0]
    cache_positions = cached_key_rows.shape[1]
    heads_width = QUERY_HEADS * HEAD_SIZE
    keys_grouped = cached_key_rows.reshape(
        sequence_rows, cache_positions, KEY_VALUE_HEADS, HEAD_SIZE
    )
    values_grouped = cached_value_rows.reshape(
        sequence_rows, cache_positions, KEY_VALUE_HEADS, HEAD_SIZE
    )
    hidden = residual
    key_collection = []
    value_collection = []
    branches = []
    for step_index in range(DECODE_STEPS):
        values_f = hidden.astype(jnp.float32)
        squares = jnp.sum(values_f * values_f, axis=1)
        totals = lax.psum(squares, "wide")
        own_squares = lax.dynamic_slice_in_dim(
            totals, lax.axis_index("wide") * sequence_rows, sequence_rows, 0
        )
        inverse = lax.rsqrt(own_squares / D + EPSILON)
        gained = (values_f * norm_gain.astype(jnp.float32)).astype(jnp.bfloat16)
        projected_rows = lax.psum_scatter(
            jnp.dot(gained, w_qkv, preferred_element_type=jnp.float32),
            "wide",
            scatter_dimension=0,
            tiled=True,
        )
        query_raw = projected_rows[:, :heads_width]
        pair_raw = projected_rows[:, heads_width:]
        token_position = lengths + step_index
        query_rows = apply_rotation(
            (query_raw * inverse[:, None]).reshape(sequence_rows, QUERY_HEADS, HEAD_SIZE),
            token_position,
        ).astype(jnp.bfloat16)
        query_rows = query_rows.reshape(
            sequence_rows, KEY_VALUE_HEADS, QUERY_HEADS // KEY_VALUE_HEADS, HEAD_SIZE
        )
        scaled_key_value = pair_raw * inverse[:, None]
        incoming_key = apply_rotation(
            scaled_key_value[:, : KEY_VALUE_HEADS * HEAD_SIZE].reshape(
                sequence_rows, KEY_VALUE_HEADS, HEAD_SIZE
            ),
            token_position,
        ).astype(jnp.bfloat16)
        incoming_value = (
            scaled_key_value[:, KEY_VALUE_HEADS * HEAD_SIZE :]
            .reshape(sequence_rows, KEY_VALUE_HEADS, HEAD_SIZE)
            .astype(jnp.bfloat16)
        )
        key_collection.append(incoming_key)
        value_collection.append(incoming_value)
        attended = attend(
            query_rows,
            keys_grouped,
            values_grouped,
            lengths,
            jnp.stack(key_collection, axis=2),
            jnp.stack(value_collection, axis=2),
        )
        mixed = jnp.dot(
            lax.all_gather(attended, "wide", axis=0, tiled=True),
            w_out,
            preferred_element_type=jnp.float32,
        ).astype(jnp.bfloat16)
        branches.append(mixed)
        hidden = (values_f + mixed.astype(jnp.float32)).astype(jnp.bfloat16)
    fresh_entries = jnp.stack(
        [
            jnp.concatenate(
                [
                    key_collection[step_number].reshape(sequence_rows, KEY_VALUE_HEADS * HEAD_SIZE),
                    value_collection[step_number].reshape(
                        sequence_rows, KEY_VALUE_HEADS * HEAD_SIZE
                    ),
                ],
                axis=1,
            )
            for step_number in range(DECODE_STEPS)
        ],
        axis=1,
    )
    return (jnp.stack(branches, axis=0), fresh_entries)


def solution(mesh):
    in_specs = (
        P("group", "wide"),
        P("wide"),
        P("wide", None),
        P(None, "wide"),
        P(("group", "wide"), None, None),
        P(("group", "wide"), None, None),
        P(("group", "wide")),
    )
    out_specs = (P(None, "group", "wide"), P(("group", "wide"), None, None))
    return jax.shard_map(shards, mesh=mesh, in_specs=in_specs, out_specs=out_specs, check_vma=False)
```

profile of v0, /device:TPU:0, one launch (start us, length us, event | category | flops | bytes accessed | tf_op | source)
XLA Modules:
  0.0 292.8 jit_solution(126512335137975647)
XLA Ops:
  7.2 0.0 copy-start
  7.2 0.0 copy-start.4
  7.2 0.0 copy-start.1
  7.2 0.0 all-reduce.5.cloned.1.call-start
  7.3 0.8 convert_element_type.117
  8.1 10.8 %fusion.29 = f32[32,9216]{1,0:T(8,128)} fusion(bf16[1024,9216]{1,0:T(8,128)(2,1)} %param.9, bf16[32,1024]{1,0:T(8,128)(2,1)} %param.7, f32[1024]{0:T(1024)S(1)} %convert_element_type.117), kind=kOutput, calls=%fused_computation.42 | convolution fusion | flops 604078080 | bytes 20123648 | tf_op jit(solution)/shard_map/dot_general | solution.py:92
  18.9 0.0 all-reduce.5.cloned.1.call-update
  18.9 0.0 all-reduce.7.cloned.1.call-start
  19.0 0.1 fusion.23
  19.1 0.6 dynamic-slice
  20.4 35.4 %psum.14 = f32[32]{0:T(128)S(1)} all-reduce(f32[32]{0:T(128)S(1)} %fusion.23), channel_id=1, replica_groups=mesh['group'=2,'wide'=16] {'wide'}, use_global_device_ids=true, to_apply=%region_2.0 | all-reduce | flops 32 | bytes 256 | tf_op jit(solution)/shard_map/psum | solution.py:85
  55.7 0.1 add_rsqrt_fusion.1
  55.8 0.1 iota_compare_fusion
  55.9 0.1 multiply_cosine_fusion
  56.0 59.6 %all-reduce.5.cloned.1.call-done = f32[32,9216]{1,0:T(8,128)} async-done(((f32[32,9216]{1,0:T(8,128)}), f32[32,9216]{1,0:T(8,128)}) %all-reduce.5.cloned.1.call-update) | async-done | bytes 1179664
  115.6 0.8 dynamic-slice_multiply_fusion.3
  116.5 1.0 fusion.34
  117.6 0.1 multiply_subtract_fusion
  117.6 0.1 subtract_convert_fusion.1
  117.7 0.1 fusion.70
  117.8 0.2 fusion.38
  118.0 0.5 fusion.60
  118.5 0.2 fusion.16
  118.8 0.3 fusion.5
  119.1 20.8 %all-gather = bf16[16,2,8192]{2,1,0:T(2,128)(2,1)S(1)} all-gather(bf16[1,2,8192]{2,1,0:T(2,128)(2,1)S(1)} %reshape.312), channel_id=1, replica_groups=mesh['group'=2,'wide'=16] {'wide'}, dimensions={0}, use_global_device_ids=true | all-gather | bytes 557056 | tf_op jit(solution)/shard_map/all_gather | solution.py:130
  139.9 0.2 reshape.313
  140.1 8.9 %fusion.21 = (f32[32]{0:T(128)S(1)}, bf16[32,1024]{1,0:T(8,128)(2,1)S(1)}) fusion(bf16[32,1024]{1,0:T(8,128)(2,1)S(1)} %copy-done.1, bf16[32,8192]{1,0:T(8,128)(2,1)S(1)} %reshape.313, bf16[8192,1024]{1,0:T(8,128)(2,1)} %param.10), kind=kOutput, calls=%fused_computation.35 | convolution fusion | flops 537133056 | bytes 17432704 | tf_op jit(solution)/shard_map/dot_general | solution.py:129
  149.0 10.8 %fusion.31 = f32[32,9216]{1,0:T(8,128)} fusion(bf16[1024,9216]{1,0:T(8,128)(2,1)} %param.9, f32[1024]{0:T(1024)S(1)} %convert_element_type.117, bf16[32,1024]{1,0:T(8,128)(2,1)S(1)} %copy-done.1, bf16[32,1024]{1,0:T(8,128)(2,1)S(1)} %get-tuple-element.33), kind=kOutput, calls=%fused_computation.43 | convolution fusion | flops 604209152 | bytes 20189184 | tf_op jit(solution)/shard_map/dot_general | solution.py:92
  159.8 0.0 all-reduce.7.cloned.1.call-update
  159.8 0.1 fusion.69
  159.9 30.1 %psum.15 = f32[32]{0:T(128)S(1)} all-reduce(f32[32]{0:T(128)S(1)} %get-tuple-element.32), channel_id=1, replica_groups=mesh['group'=2,'wide'=16] {'wide'}, use_global_device_ids=true, to_apply=%region_7.8 | all-reduce | flops 32 | bytes 256 | tf_op jit(solution)/shard_map/psum | solution.py:85
  190.0 0.1 add_rsqrt_fusion
  190.1 60.9 %all-reduce.7.cloned.1.call-done = f32[32,9216]{1,0:T(8,128)} async-done(((f32[32,9216]{1,0:T(8,128)}), f32[32,9216]{1,0:T(8,128)}) %all-reduce.7.cloned.1.call-update) | async-done | bytes 1179664
  251.0 0.8 dynamic-slice_multiply_fusion.2
  251.8 0.1 subtract_convert_fusion.2
  251.9 0.1 maximum_bitcast_fusion.2
  252.0 1.0 fusion.33
  253.1 0.1 subtract_convert_fusion
  253.2 0.5 fusion.61
  253.7 0.2 fusion.62
  253.9 0.2 fusion.18
  254.1 0.3 fusion.7
  254.5 0.6 copy.57
  255.1 0.2 fusion.6
  255.4 21.0 %all-gather.1 = bf16[16,2,8192]{2,1,0:T(2,128)(2,1)S(1)} all-gather(bf16[1,2,8192]{2,1,0:T(2,128)(2,1)S(1)} %reshape.314), channel_id=1, replica_groups=mesh['group'=2,'wide'=16] {'wide'}, dimensions={0}, use_global_device_ids=true | all-gather | bytes 557056 | tf_op jit(solution)/shard_map/all_gather | solution.py:130
  276.3 0.2 reshape.315
  276.5 8.7 %fusion.2 = bf16[1,32,1024]{2,1,0:T(8,128)(2,1)S(1)} fusion(bf16[32,8192]{1,0:T(8,128)(2,1)S(1)} %reshape.315, bf16[8192,1024]{1,0:T(8,128)(2,1)} %param.10), kind=kOutput, calls=%fused_computation.6 | convolution fusion | flops 536903680 | bytes 17367040 | tf_op jit(solution)/shard_map/dot_general | solution.py:129
  285.3 0.7 pad_maximum_fusion
  (35 shorter events, 0.3 us)
Async XLA Ops:
  7.2 110.9 %copy-start = (bf16[2,512,512]{2,1,0:T(8,128)(2,1)S(1)}, bf16[2,512,512]{2,1,0:T(8,128)(2,1)}, u32[]{:S(2)}) copy-start(bf16[2,512,512]{2,1,0:T(8,128)(2,1)} %param.11) | copy-start | bytes 3145732
  7.2 12.0 %copy-start.4 = (u32[32]{0:T(128)S(1)}, u32[32]{0:T(128)}, u32[]{:S(2)}) copy-start(u32[32]{0:T(128)} %constant.35) | copy-start | bytes 388
  7.2 11.8 %copy-start.1 = (bf16[32,1024]{1,0:T(8,128)(2,1)S(1)}, bf16[32,1024]{1,0:T(8,128)(2,1)}, u32[]{:S(2)}) copy-start(bf16[32,1024]{1,0:T(8,128)(2,1)} %param.7) | copy-start | bytes 196612
  7.2 11.9 %copy-start.3 = (s32[2]{0:T(128)S(1)}, s32[2]{0:T(128)}, u32[]{:S(2)}) copy-start(s32[2]{0:T(128)} %param.13) | copy-start | bytes 28
  7.2 111.6 %copy-start.2 = (bf16[2,512,512]{2,1,0:T(8,128)(2,1)S(1)}, bf16[2,512,512]{2,1,0:T(8,128)(2,1)}, u32[]{:S(2)}) copy-start(bf16[2,512,512]{2,1,0:T(8,128)(2,1)} %param.12) | copy-start | bytes 3145732
  7.2 108.4 %all-reduce.5.cloned.1.call-start = ((), (), s32[]{:S(2)}) async-start(), calls=%async_computation | async-start | bytes 2359296
  18.9 232.1 %all-reduce.7.cloned.1.call-start = ((), (), s32[]{:S(2)}) async-start(), calls=%async_computation.1 | async-start | bytes 2359296
Sparse Core Ops, SparseCore 0:
  19.0 96.5 all-reduce.4
  159.9 90.9 all-reduce.6
where the time goes:
time: 293 us
  waiting for transfers between devices  121 us (41%)
  blocking collectives  107 us (37%)
  matrix products  41.5 us (14%)
  between operations  15 us (5%)
  other arithmetic  6.79 us (2%)
    unnamed x4, waiting for transfers between devices  121 us
    psum x2, blocking collectives, shards(): totals = lax.psum(squares, 'wide')  65.5 us
    all_gather x2, blocking collectives, shards(): lax.all_gather(attended, 'wide', axis=0, tiled=True)  41.7 us
    dot_general x2, matrix products, shards(): jnp.dot(gained, w_qkv, preferred_element_type=jnp.float32)  21.6 us
    dot_general x2, matrix products, shards(): jnp.dot(lax.all_gather(attended, 'wide', axis=0, tiled=True), w_out, pref...  17.6 us
  transfers between devices with their start and end apart: 2, of which 2 were waited for; matrix products, arithmetic and copies ran while one was open for 0% of the time, Pallas kernels for 0%

commit v1 on v0

v1 whole, which is shorter than its diff:
```python
import jax
import jax.numpy as jnp
from jax import lax
from jax.experimental import pallas as pl
from jax.experimental.pallas import tpu as pltpu
from jax.sharding import PartitionSpec as P

QUERY_HEADS = 64
KEY_VALUE_HEADS = 4
HEAD_SIZE = 128
DECODE_STEPS = 2
EPSILON = 1e-05
ROPE_BASE = 500000.0

GROUP_HEADS = QUERY_HEADS // KEY_VALUE_HEADS
HEADS_WIDTH = QUERY_HEADS * HEAD_SIZE
PAIR_HEADS = 2 * KEY_VALUE_HEADS
CHUNKS = [(QUERY_HEADS, PAIR_HEADS)] + [
    (k * GROUP_HEADS, GROUP_HEADS) for k in range(KEY_VALUE_HEADS)
]
ROW0 = [0] + [2 * PAIR_HEADS + 2 * k * GROUP_HEADS for k in range(KEY_VALUE_HEADS)]
LAST_CHUNK = len(CHUNKS) - 1
MESSAGE_ROWS = 2 * (QUERY_HEADS + PAIR_HEADS)
TILE = 512
MESH = pl.DeviceIdType.MESH
F32 = jnp.float32
BF16 = jnp.bfloat16


def semaphore_names(depth):
    names = []
    for t in range(DECODE_STEPS):
        names += [("q", t, 1), ("q", t, 2)]
        names += [("q", t, 3, r) for r in range(1, depth)]
        for j in range(len(CHUNKS)):
            names += [("p", t, j, 1), ("p", t, j, 2)]
            names += [("p", t, j, 3, r) for r in range(1, depth)]
        names += [("p", t, LAST_CHUNK, 3, r) for r in range(depth, 2 * depth)]
        for k in range(KEY_VALUE_HEADS):
            names += [("g", t, k, 2), ("g", t, k, 1)]
            names += [("g", t, k, 3, r) for r in range(1, depth)]
        names += [("g", t, LAST_CHUNK - 1, 3, r) for r in range(depth, 2 * depth)]
    return {name: index for index, name in enumerate(names)}


def make_kernel(n):
    depth = n // 4
    rows = 2 * n
    half = n
    quarter = n // 2
    sems = semaphore_names(depth)
    block = 2 * GROUP_HEADS

    def kernel(
        len_ref, x_ref, gain_ref, wq_hbm, wo_hbm, k_hbm, v_hbm,
        branch_ref, fresh_ref,
        wq, wo, keys, values,
        own, s1, r1, s2, r2, folded, s3, r3,
        sq, gathered, wide_f, lhs, acc, hidden,
        load_sem, send_sem, recv_sem,
    ):
        me = lax.axis_index("wide")
        my_a = me // 4
        my_b = (me // 2) % 2
        my_c = me % 2
        core_peer = {"wide": my_a * 4 + my_b * 2 + (1 - my_c)}
        y_peer = {"wide": my_a * 4 + (1 - my_b) * 2 + my_c}
        z_peer = [
            {"wide": lax.rem(my_a + r, depth) * 4 + my_b * 2 + my_c} for r in range(depth)
        ] + [
            {"wide": lax.rem(my_a + r, depth) * 4 + (1 - my_b) * 2 + my_c} for r in range(depth)
        ]
        there = [(depth - r) % depth for r in range(depth)]
        there += [depth + r for r in there]

        def wq_copy(j):
            head, count = CHUNKS[j]
            columns = pl.ds(head * HEAD_SIZE, count * HEAD_SIZE)
            return pltpu.make_async_copy(wq_hbm.at[:, columns], wq.at[:, columns], load_sem.at[j])

        def wo_copy(k):
            part = pl.ds(k * GROUP_HEADS * HEAD_SIZE, GROUP_HEADS * HEAD_SIZE)
            return pltpu.make_async_copy(wo_hbm.at[part], wo.at[part], load_sem.at[7 + k])

        key_copy = pltpu.make_async_copy(k_hbm, keys, load_sem.at[5])
        value_copy = pltpu.make_async_copy(v_hbm, values, load_sem.at[6])
        for j in range(len(CHUNKS)):
            wq_copy(j).start()

        barrier = pltpu.get_barrier_semaphore()
        for peer in [core_peer] + z_peer[1:]:
            pl.semaphore_signal(barrier, inc=1, device_id=peer, device_id_type=MESH)

        copies = {}

        def send(name, src, dst, peer):
            copy = pltpu.make_async_remote_copy(
                src_ref=src,
                dst_ref=dst,
                send_sem=send_sem.at[sems[name]],
                recv_sem=recv_sem.at[sems[name]],
                device_id=peer,
                device_id_type=MESH,
            )
            copy.start()
            copies[name] = copy

        position = lax.broadcasted_iota(jnp.int32, (rows, rows), 0)
        natural = lax.broadcasted_iota(jnp.int32, (rows, rows), 1)
        s_pos = position % 2
        a_pos = (my_a + (position // 2) % depth) % depth
        b_pos = (my_b + (position // quarter) % 2) % 2
        c_pos = (my_c + position // half) % 2
        row_of = 2 * (4 * a_pos + 2 * b_pos + c_pos) + s_pos
        arrange = (row_of == natural).astype(F32).astype(BF16)
        diagonal = position == natural

        lane = lax.broadcasted_iota(jnp.int32, (1, HEAD_SIZE), 1)
        pair = lane % (HEAD_SIZE // 2)
        frequency = jnp.ones((1, HEAD_SIZE), F32)
        for bit in range(6):
            factor = ROPE_BASE ** (-(2.0 ** (bit + 1)) / HEAD_SIZE)
            frequency = frequency * jnp.where((pair // 2**bit) % 2 == 1, F32(factor), F32(1.0))
        tables = {}
        for t in range(DECODE_STEPS):
            for s in range(2):
                angle = (len_ref[s] + t).astype(F32) * frequency
                sine = jnp.sin(angle)
                tables[t, s] = (
                    jnp.cos(angle),
                    jnp.where(lane < HEAD_SIZE // 2, -sine, sine),
                )

        def rotate(vectors, t, s):
            cosine, sine = tables[t, s]
            return vectors * cosine + pltpu.roll(vectors, HEAD_SIZE // 2, 1) * sine

        slot = lax.broadcasted_iota(jnp.int32, (GROUP_HEADS, keys.shape[1]), 1)
        fresh_keys, fresh_values = {}, {}
        inverse = {}
        width = x_ref.shape[1] * n

        hidden[...] = x_ref[...]

        def start_step(t):
            x = hidden[...].astype(F32)
            squares = jnp.sum(x * x, axis=1, keepdims=True)
            line = jnp.sum(jnp.where(diagonal, squares, 0.0), axis=0, keepdims=True)
            if rows < HEAD_SIZE:
                line = jnp.concatenate([line] + [jnp.zeros((1, HEAD_SIZE - rows), F32)], axis=1)
            sq[t, 0] = jnp.broadcast_to(line, (8, HEAD_SIZE))
            gained = (x * gain_ref[...].astype(F32).reshape(1, -1)).astype(BF16)
            return jnp.dot(arrange, gained, preferred_element_type=F32).astype(BF16)

        def project(t, j, gained):
            head, count = CHUNKS[j]
            if t == 0:
                wq_copy(j).wait()

            def body(i, carry):
                columns = pl.ds(pl.multiple_of(head * HEAD_SIZE + i * TILE, TILE), TILE)
                part = jnp.dot(gained, wq[:, columns], preferred_element_type=F32)
                own[:, columns] = part[:half]
                s1[t, :, columns] = part[half:].astype(BF16)
                return carry

            lax.fori_loop(0, count * HEAD_SIZE // TILE, body, 0, unroll=2)
            if t == 0 and j == 0:
                pl.semaphore_wait(barrier, 2 * depth)
            if j == 0:
                send(("q", t, 1), sq.at[t, 0], sq.at[t, 1], core_peer)
            columns = pl.ds(head * HEAD_SIZE, count * HEAD_SIZE)
            send(("p", t, j, 1), s1.at[t, :, columns], r1.at[t, :, columns], core_peer)

        def send_sum(t, j, r):
            count = CHUNKS[j][1]
            place = pl.ds(ROW0[j], 2 * count)
            start = 2 * (r % depth)
            s3[t, r, place, :] = jnp.concatenate(
                [
                    folded[j + r // depth, pl.ds(start + s, count, stride=quarter), :]
                    for s in range(2)
                ],
                axis=0,
            ).astype(BF16)
            send(("p", t, j, 3, r), s3.at[t, r, place], r3.at[t, there[r], place], z_peer[r])

        def reduce_core(t, j):
            head, count = CHUNKS[j]
            if j == 0:
                copies["q", t, 1].wait_recv()
                sq[t, 2] = sq[t, 0] + sq[t, 1]
                send(("q", t, 2), sq.at[t, 2], sq.at[t, 3], y_peer)
            copies["p", t, j, 1].wait_recv()
            first, size = head * HEAD_SIZE, count * HEAD_SIZE
            columns = pl.ds(first, size)
            total = own[:, columns] + r1[t, :, columns].astype(F32)
            if j == LAST_CHUNK:
                for side in range(2):
                    for h in range(count):
                        folded[j + side, pl.ds(h * quarter, quarter), :] = total[
                            side * quarter : (side + 1) * quarter,
                            h * HEAD_SIZE : (h + 1) * HEAD_SIZE,
                        ]
                for r in range(depth, 2 * depth):
                    send_sum(t, j, r)
                for r in range(1, depth):
                    send_sum(t, j, r)
                return
            own[0:quarter, columns] = total[:quarter]
            away = total[quarter:]
            packed = pl.ds(first // 2, size // 2)
            s2[t, :, packed] = jnp.concatenate(
                [away[:, : size // 2], away[:, size // 2 :]], axis=0
            ).astype(BF16)
            send(("p", t, j, 2), s2.at[t, :, packed], r2.at[t, :, packed], y_peer)

        def reduce_y(t, j):
            head, count = CHUNKS[j]
            if j == 0:
                copies["q", t, 2].wait_recv()
                sq[t, 4] = sq[t, 2] + sq[t, 3]
                for r in range(1, depth):
                    send(("q", t, 3, r), sq.at[t, 4], sq.at[t, 4 + depth - r], z_peer[r])
            copies["p", t, j, 2].wait_recv()
            first, size = head * HEAD_SIZE, count * HEAD_SIZE
            arrived = r2[t, :, pl.ds(first // 2, size // 2)].astype(F32)
            for h in range(count):
                place = h * HEAD_SIZE
                if place < size // 2:
                    other = arrived[:quarter, place : place + HEAD_SIZE]
                else:
                    place -= size // 2
                    other = arrived[quarter:, place : place + HEAD_SIZE]
                folded[j, pl.ds(h * quarter, quarter), :] = (
                    own[0:quarter, pl.ds(first + h * HEAD_SIZE, HEAD_SIZE)] + other
                )
            for r in range(1, depth):
                send_sum(t, j, r)

        def reduce_z(t, j):
            head, count = CHUNKS[j]
            if j == 0:
                total = sq[t, 4]
                for r in range(1, depth):
                    copies["q", t, 3, r].wait_recv()
                for r in range(1, depth):
                    total = total + sq[t, 4 + r]
                line = total[0:1]
                for s in range(2):
                    mine = jnp.sum(
                        jnp.where(lane == 2 * me + s, line, 0.0), axis=1, keepdims=True
                    )
                    inverse[t, s] = lax.rsqrt(mine / width + EPSILON)
            others = range(1, 2 * depth if j == LAST_CHUNK else depth)
            for r in others:
                copies["p", t, j, 3, r].wait_recv()
            arrived = None
            for r in others:
                term = r3[t, r, pl.ds(ROW0[j], 2 * count), :].astype(F32)
                arrived = term if arrived is None else arrived + term
            result = []
            for s in range(2):
                mine = folded[j, pl.ds(s, count, stride=quarter), :]
                result.append((mine + arrived[s * count : (s + 1) * count]) * inverse[t, s])
            return result

        def finish_pair(t):
            both = reduce_z(t, 0)
            for s in range(2):
                rotated = rotate(both[s], t, s)
                fresh_keys[t, s] = rotated[:KEY_VALUE_HEADS].astype(BF16).astype(F32)
                fresh_values[t, s] = both[s][KEY_VALUE_HEADS:].astype(BF16).astype(F32)

        def attend(t, k):
            queries = reduce_z(t, k + 1)
            if t == 0 and k == 0:
                key_copy.wait()
                value_copy.wait()
            scaling = 1.0 / HEAD_SIZE**0.5
            columns = pl.ds(k * HEAD_SIZE, HEAD_SIZE)
            results = []
            for s in range(2):
                query = rotate(queries[s], t, s).astype(BF16)
                scores = lax.dot_general(
                    query, keys[s, :, columns], (((1,), (1,)), ((), ())),
                    preferred_element_type=F32,
                ) * scaling
                scores = jnp.where(slot < len_ref[s], scores, -jnp.inf)
                query_f = query.astype(F32)
                recent = [
                    jnp.sum(query_f * fresh_keys[u, s][k : k + 1], axis=1, keepdims=True) * scaling
                    for u in range(t + 1)
                ]
                peak = jnp.max(scores, axis=1, keepdims=True)
                for score in recent:
                    peak = jnp.maximum(peak, score)
                e = jnp.exp(scores - peak)
                denominator = jnp.sum(e, axis=1, keepdims=True)
                weighted = jnp.dot(e.astype(BF16), values[s, :, columns], preferred_element_type=F32)
                for u, score in enumerate(recent):
                    e_new = jnp.exp(score - peak)
                    denominator = denominator + e_new
                    weighted = (
                        weighted + e_new.astype(BF16).astype(F32) * fresh_values[u, s][k : k + 1]
                    )
                results.append(weighted / denominator)
            gathered[t, k, pl.ds(0, block), :] = jnp.concatenate(results, axis=0).astype(BF16)
            for r in range(1, 2 * depth if k + 1 == LAST_CHUNK else depth):
                send(
                    ("g", t, k, 3, r),
                    gathered.at[t, k, pl.ds(0, block)],
                    gathered.at[t, k, pl.ds(there[r] * block, block)],
                    z_peer[r],
                )

        def gather_y(t, k):
            for r in range(1, depth):
                copies["g", t, k, 3, r].wait_recv()
            size = depth * block
            send(
                ("g", t, k, 2),
                gathered.at[t, k, pl.ds(0, size)],
                gathered.at[t, k, pl.ds(size, size)],
                y_peer,
            )

        def gather_core(t, k):
            if k + 1 == LAST_CHUNK:
                for r in range(1, 2 * depth):
                    copies["g", t, k, 3, r].wait_recv()
            else:
                copies["g", t, k, 2].wait_recv()
            size = 2 * depth * block
            send(
                ("g", t, k, 1),
                gathered.at[t, k, pl.ds(0, size)],
                gathered.at[t, k, pl.ds(size, size)],
                core_peer,
            )

        def output(t, k):
            copies["g", t, k, 1].wait_recv()
            if t == 0:
                wo_copy(k).wait()
            wide_f[...] = gathered[t, k].astype(F32)
            for h in range(GROUP_HEADS):
                lhs[:, pl.ds(h * HEAD_SIZE, HEAD_SIZE)] = wide_f[
                    pl.ds(h, rows, stride=GROUP_HEADS), :
                ].astype(BF16)
            part = GROUP_HEADS * HEAD_SIZE
            tile = min(512, x_ref.shape[1])

            def body(i, carry):
                columns = pl.ds(pl.multiple_of(i * tile, tile), tile)
                term = jnp.dot(
                    lhs[...], wo[pl.ds(k * part, part), columns], preferred_element_type=F32
                )
                if k:
                    term = acc[:, columns] + term
                acc[:, columns] = term
                return carry

            lax.fori_loop(0, x_ref.shape[1] // tile, body, 0, unroll=True)

        def finish_step(t):
            mixed = acc[...].astype(BF16)
            natural_order = lax.dot_general(
                arrange, mixed, (((0,), (0,)), ((), ())), preferred_element_type=F32
            )
            branch_ref[t] = natural_order.astype(BF16)
            hidden[...] = (hidden[...].astype(F32) + natural_order).astype(BF16)

        for t in range(DECODE_STEPS):
            gained = start_step(t)
            project(t, 0, gained)
            project(t, 1, gained)
            reduce_core(t, 0)
            project(t, 2, gained)
            if t == 0:
                key_copy.start()
                value_copy.start()
                for k in range(KEY_VALUE_HEADS):
                    wo_copy(k).start()
            reduce_core(t, 1)
            project(t, 3, gained)
            reduce_core(t, 2)
            if t == 0:
                reduce_y(t, 0)
            project(t, 4, gained)
            reduce_core(t, 3)
            if t > 0:
                reduce_y(t, 0)
            reduce_core(t, 4)
            reduce_y(t, 1)
            reduce_y(t, 2)
            finish_pair(t)
            reduce_y(t, 3)
            attend(t, 0)
            attend(t, 1)
            gather_y(t, 0)
            attend(t, 2)
            gather_y(t, 1)
            attend(t, 3)
            gather_y(t, 2)
            gather_core(t, 0)
            gather_core(t, 1)
            output(t, 0)
            gather_core(t, 2)
            output(t, 1)
            gather_core(t, 3)
            output(t, 2)
            output(t, 3)
            finish_step(t)

        for s in range(2):
            lines = []
            for t in range(DECODE_STEPS):
                pieces = [
                    part[h : h + 1]
                    for part in (fresh_keys[t, s], fresh_values[t, s])
                    for h in range(KEY_VALUE_HEADS)
                ]
                lines.append(jnp.concatenate(pieces, axis=1))
            fresh_ref[s] = jnp.concatenate(lines, axis=0).astype(BF16)
        for copy in copies.values():
            copy.wait_send()

    return kernel, len(sems)


def solution(mesh):
    n = mesh.shape["wide"]
    depth = n // 4
    kernel, copies = make_kernel(n)

    def shards(residual, norm_gain, w_qkv, w_out, cached_key_rows, cached_value_rows, lengths):
        rows, width = residual.shape
        sequences = lengths.shape[0]
        columns = w_qkv.shape[1]
        chunks = len(CHUNKS)
        vmem = pl.BlockSpec(memory_space=pltpu.VMEM)
        hbm = pl.BlockSpec(memory_space=pl.ANY)
        branch, fresh = pl.pallas_call(
            kernel,
            out_shape=(
                jax.ShapeDtypeStruct((DECODE_STEPS, rows, width), BF16),
                jax.ShapeDtypeStruct((sequences, DECODE_STEPS, PAIR_HEADS * HEAD_SIZE), BF16),
            ),
            in_specs=[pl.BlockSpec(memory_space=pltpu.SMEM), vmem, vmem, hbm, hbm, hbm, hbm],
            out_specs=(vmem, vmem),
            scratch_shapes=[
                pltpu.VMEM(w_qkv.shape, BF16),
                pltpu.VMEM(w_out.shape, BF16),
                pltpu.VMEM(cached_key_rows.shape, BF16),
                pltpu.VMEM(cached_value_rows.shape, BF16),
                pltpu.VMEM((rows // 2, columns), F32),
                pltpu.VMEM((DECODE_STEPS, rows // 2, columns), BF16),
                pltpu.VMEM((DECODE_STEPS, rows // 2, columns), BF16),
                pltpu.VMEM((DECODE_STEPS, rows // 2, columns // 2), BF16),
                pltpu.VMEM((DECODE_STEPS, rows // 2, columns // 2), BF16),
                pltpu.VMEM((chunks + 1, GROUP_HEADS * rows // 4, HEAD_SIZE), F32),
                pltpu.VMEM((DECODE_STEPS, 2 * depth, MESSAGE_ROWS, HEAD_SIZE), BF16),
                pltpu.VMEM((DECODE_STEPS, 2 * depth, MESSAGE_ROWS, HEAD_SIZE), BF16),
                pltpu.VMEM((DECODE_STEPS, 4 + depth, 8, HEAD_SIZE), F32),
                pltpu.VMEM(
                    (DECODE_STEPS, KEY_VALUE_HEADS, rows * GROUP_HEADS, HEAD_SIZE), BF16
                ),
                pltpu.VMEM((rows * GROUP_HEADS, HEAD_SIZE), F32),
                pltpu.VMEM((rows, GROUP_HEADS * HEAD_SIZE), BF16),
                pltpu.VMEM((rows, width), F32),
                pltpu.VMEM((rows, width), BF16),
                pltpu.SemaphoreType.DMA((11,)),
                pltpu.SemaphoreType.DMA((copies,)),
                pltpu.SemaphoreType.DMA((copies,)),
            ],
            compiler_params=pltpu.CompilerParams(
                collective_id=0, has_side_effects=True, vmem_limit_bytes=56 * 1024 * 1024
            ),
            name="decode",
        )(
            lengths,
            residual,
            norm_gain,
            w_qkv,
            w_out,
            cached_key_rows,
            cached_value_rows,
        )
        return branch, fresh

    in_specs = (
        P("group", "wide"),
        P("wide"),
        P("wide", None),
        P(None, "wide"),
        P(("group", "wide"), None, None),
        P(("group", "wide"), None, None),
        P(("group", "wide")),
    )
    out_specs = (P(None, "group", "wide"), P(("group", "wide"), None, None))
    return jax.shard_map(shards, mesh=mesh, in_specs=in_specs, out_specs=out_specs, check_vma=False)
```

time: 293 us -> 62 us (0.21)
  waiting for transfers between devices: 121 us -> 0 us
  blocking collectives: 107 us -> 0 us
  Pallas kernels: 0 us -> 58.2 us
  matrix products: 41.5 us -> 0 us
  between operations: 15 us -> 0.64 us
  other arithmetic: 6.79 us -> 0 us
    unnamed x4 -> x0, waiting for transfers between devices: 121 us -> none
    psum x2 -> x0, blocking collectives: 65.5 us -> none  [shards(): totals = lax.psum(squares, 'wide')]
    pallas_call x0 -> x1, Pallas kernels: none -> 58.2 us  [shards(): pl.pallas_call(kernel, out_shape=(jax.ShapeDtypeStruct((DECODE_STEPS, row...]
    all_gather x2 -> x0, blocking collectives: 41.7 us -> none  [shards(): lax.all_gather(attended, 'wide', axis=0, tiled=True)]
    dot_general x11 -> x0, matrix products: 41.5 us -> none  [the longest x2 21.6 us: shards(): jnp.dot(gained, w_qkv, preferred_element_type=jnp.float32)]
  transfers between devices with their start and end apart: 2 -> 0, of which waited for: 2 -> 0; matrix products, arithmetic and copies ran while one was open for 0% -> 0% of each run, Pallas kernels for 0% -> 0%
where the time goes in v1:
time: 62 us; the launch traced here: 61.7 us
  Pallas kernels  58.2 us (94%)
  local copies, waits for them, and re-layouts  2.87 us (5%)
  between operations  0.64 us (1%)
    pallas_call x1, Pallas kernels, shards(): pl.pallas_call(kernel, out_shape=(jax.ShapeDtypeStruct((DECODE_STEPS, row...  58.2 us
    unnamed x2, local copies, waits for them, and re-layouts  2.87 us

profile of v1, /device:TPU:0, one launch (start us, length us, event | category | flops | bytes accessed | tf_op | source)
XLA Modules:
  0.0 61.7 jit_solution(14727897569703822639)
XLA Ops:
  0.6 58.2 %decode.1 = (bf16[2,32,1024]{2,1,0:T(8,128)(2,1)}, bf16[2,2,1024]{2,1,0:T(2,128)(2,1)}) custom-call(s32[2]{0:T(128)} %len_ref.1, bf16[32,1024]{1,0:T(8,128)(2,1)} %x_ref.1, bf16[1024]{0:T(1024)(128)(2,1)} %gain_ref.1, bf16[1024,9216]{1,0:T(8,128)(2,1)} %wq_hbm.1, bf16[8192,1024]{1,0:T(8,128)(2,1)} %wo_hbm.1, bf16[2,512,512]{2,1,0:T(8,128)(2,1)} %k_hbm.1, ...), custom_call_target="tpu_custom_call" | custom-call | tf_op jit(solution)/shard_map/decode/pallas_call | solution.py:444
  58.9 1.6 %copy.11 = bf16[2,32,1024]{2,1,0:T(8,128)(2,1)} copy(bf16[2,32,1024]{2,1,0:T(8,128)(2,1)} %get-tuple-element.4) | data formatting | bytes 262144
  60.4 1.3 %copy.12 = bf16[2,2,1024]{2,1,0:T(2,128)(2,1)} copy(bf16[2,2,1024]{2,1,0:T(2,128)(2,1)} %get-tuple-element.5) | data formatting | bytes 16384
